TPU v7x, 256 devices: a whole 4x4x8 slice. The times are simulated.
256 devices in a mesh: context: 16 (over y_hi, z), tensor: 8 (over x, y_lo), dp: 2 (over core).
Axes of the slice: x: 4, y: 4 (y_hi: 2, y_lo: 2; y = y_hi * 2 + y_lo), z: 8, core: 2. Of those that a mesh axis runs over, the one named last changes fastest.
Arguments:
- turn_q: bfloat16 [16384, 8192], P(('dp', 'context'), 'tensor'), parts along dimension 0, may hold values from -5 to 5
- new_turn_keys: bfloat16 [16384, 1024], P(('dp', 'context'), 'tensor'), parts along dimension 0, may hold values from -5 to 5
- new_turn_values: bfloat16 [16384, 1024], P(('dp', 'context'), 'tensor'), parts along dimension 0, may hold values from -6 to 6
- block_mask: int32 [16, 16], replicated, may hold values from 0 to 1, as said below
- query_dec: bfloat16 [32, 4, 8192], P('dp', None, 'tensor'), parts along dimension 0, may hold values from -5 to 5
- cache_keys: bfloat16 [32, 16384, 1024], P('dp', 'context', 'tensor'), parts along dimension 0, may hold values from -5 to 5
- stream_cache_values: bfloat16 [32, 16384, 1024], P('dp', 'context', 'tensor'), parts along dimension 0, may hold values from -6 to 6
- hist_lengths: int32 [32], P('dp'), parts along dimension 0, may hold values from 1 to 16380, as said below
Outputs:
- turn_out: bfloat16 [16384, 8192], P(('dp', 'context'), 'tensor'), parts along dimension 0
- stream_out: bfloat16 [32, 4, 8192], P(('dp', 'context'), None, 'tensor'), parts along dimension 0
There are 2 independent parts, one for each index of `dp`. A program takes and returns all parts, laid end to end along the dimension named above; an argument that names none is the same for every part. Nothing has to cross between parts.
Inputs may be any that keep to these rules, and one draw needn't show every extreme that they name: `block_mask`: zero above the diagonal; one on the diagonal and in column 0; in each row the ones outside column 0 form a run that ends at the diagonal and spans at most 4 blocks, and in some row it spans exactly 4. `hist_lengths`: at least one stream has the largest value.
All inputs are finite; a program needn't handle non-finite values.
Results may differ from a plain program's by a relative error of at most 0.019.
Values may be sent and summed in bfloat16 or wider, within the bound.
A program may use at most 64 MiB of HBM per device.

v0:
```python
import math

import jax
import jax.numpy as jnp
from jax import lax
from jax.sharding import PartitionSpec as P

QUERY_HEADS = 64
KEY_VALUE_HEADS = 8
HEAD_SIZE = 128


MASKED_SCORE = -1e30


def merged(x, axis, join):
    gathered = jax.tree.map(
        lambda a, kind: lax.all_gather(a.astype(kind), axis),
        x,
        (jnp.bfloat16, jnp.bfloat16, jnp.bfloat16),
    )

    def take(source):
        return jax.tree.map(
            lambda a, own: lax.dynamic_index_in_dim(a, source, 0, False).astype(own.dtype),
            gathered,
            x,
        )

    return lax.fori_loop(
        1, lax.axis_size(axis), lambda source, state: join(state, take(source)), take(0)
    )


def attend_rows(
    carried_state,
    query_matrix,
    rows_of_keys,
    rows_of_values,
    key_start,
    query_block,
    mask_row,
    enabled,
):
    row_count = rows_of_keys.shape[0]
    query_count = query_matrix.shape[0]
    kv_heads = query_matrix.shape[1]
    key_pos = key_start + jnp.arange(row_count, dtype=jnp.int32)
    key_block = key_pos // query_count
    blocks = mask_row.shape[0]
    matches = key_block[:, None] == jnp.arange(blocks, dtype=jnp.int32)[None, :]
    picked_rows = jnp.sum(jnp.where(matches, mask_row[None, :], 0), axis=1) > 0
    query_pos = query_block * query_count + jnp.arange(query_count, dtype=jnp.int32)
    usable = picked_rows[None, :] & (
        (key_block[None, :] < query_block) | (key_pos[None, :] <= query_pos[:, None])
    )

    def attend_live(current):
        highest, weight_sum, weighted = current
        heads_of_keys = rows_of_keys.reshape(row_count, kv_heads, HEAD_SIZE)
        heads_of_values = rows_of_values.reshape(row_count, kv_heads, HEAD_SIZE)
        scores = jnp.einsum(
            "qhgd,khd->hgqk", query_matrix, heads_of_keys, preferred_element_type=jnp.float32
        ) * HEAD_SIZE ** (-0.5)
        scores = jnp.where(usable, scores, MASKED_SCORE)
        new_highest = jnp.maximum(highest, jnp.max(scores, axis=-1))
        weights = jnp.where(usable, jnp.exp(scores - new_highest[..., None]), 0.0)
        shrink = jnp.exp(highest - new_highest)
        weight_sum = weight_sum * shrink + jnp.sum(weights, axis=-1)
        weighted = weighted * shrink[..., None] + jnp.einsum(
            "hgqk,khd->hgqd",
            weights.astype(jnp.bfloat16),
            heads_of_values,
            preferred_element_type=jnp.float32,
        )
        return (new_highest, weight_sum, weighted)

    def keep_state(current):
        return current

    return lax.cond(enabled & jnp.any(usable), attend_live, keep_state, carried_state)


def attend_block(
    carried_state, query_matrix, rows_of_keys, rows_of_values, query_block, mask_row, enabled
):
    row_count = rows_of_keys.shape[0]
    piece_rows = math.gcd(row_count, 512)
    pieces = row_count // piece_rows
    key_parts = rows_of_keys.reshape(pieces, piece_rows, rows_of_keys.shape[1])
    value_parts = rows_of_values.reshape(pieces, piece_rows, rows_of_values.shape[1])

    def visitor(current, element):
        piece_index, key_piece, value_piece = element
        updated = attend_rows(
            current,
            query_matrix,
            key_piece,
            value_piece,
            piece_index * piece_rows,
            query_block,
            mask_row,
            enabled,
        )
        return (updated, None)

    carried_state, unused = lax.scan(
        visitor, carried_state, (jnp.arange(pieces, dtype=jnp.int32), key_parts, value_parts)
    )
    return carried_state


def turn_attention(turn_q, new_turn_keys, new_turn_values, block_mask):
    shard_index = lax.axis_index("context")
    query_count = turn_q.shape[0]
    kv_heads = new_turn_keys.shape[1] // HEAD_SIZE
    query_groups = QUERY_HEADS // KEY_VALUE_HEADS
    query_matrix = turn_q.reshape(query_count, kv_heads, query_groups, HEAD_SIZE)
    mask_row = lax.dynamic_index_in_dim(block_mask, shard_index, 0, keepdims=False)
    carried_state = (
        jnp.full((kv_heads, query_groups, query_count), MASKED_SCORE, jnp.float32),
        jnp.zeros((kv_heads, query_groups, query_count), jnp.float32),
        jnp.zeros((kv_heads, query_groups, query_count, HEAD_SIZE), jnp.float32),
    )
    carried_state = attend_block(
        carried_state,
        query_matrix,
        lax.all_gather(new_turn_keys, "context", axis=0, tiled=True),
        lax.all_gather(new_turn_values, "context", axis=0, tiled=True),
        shard_index,
        mask_row,
        shard_index >= 0,
    )
    highest, weight_sum, weighted = carried_state
    result = weighted / weight_sum[..., None]
    return (
        result.transpose(2, 0, 1, 3)
        .reshape(query_count, kv_heads * query_groups * HEAD_SIZE)
        .astype(jnp.bfloat16)
    )


def combine_partial(earlier, later):
    highest = jnp.maximum(earlier[0], later[0])
    scale_one = jnp.exp(earlier[0] - highest)
    scale_two = jnp.exp(later[0] - highest)
    weight_sum = earlier[1] * scale_one + later[1] * scale_two
    weighted = earlier[2] * scale_one[..., None] + later[2] * scale_two[..., None]
    return (highest, weight_sum, weighted)


def stream_attention(query_dec, cache_keys, stream_cache_values, hist_lengths):
    shard_index = lax.axis_index("context")
    context_size = lax.axis_size("context")
    streams, tokens, width_all = query_dec.shape
    positions_here = cache_keys.shape[1]
    kv_heads = cache_keys.shape[2] // HEAD_SIZE
    query_groups = QUERY_HEADS // KEY_VALUE_HEADS
    query_matrix = query_dec.reshape(streams, tokens, kv_heads, query_groups, HEAD_SIZE)
    heads_of_keys = cache_keys.reshape(streams, positions_here, kv_heads, HEAD_SIZE)
    heads_of_values = stream_cache_values.reshape(streams, positions_here, kv_heads, HEAD_SIZE)
    scores = jnp.einsum(
        "sthgd,sphd->shgtp", query_matrix, heads_of_keys, preferred_element_type=jnp.float32
    ) * HEAD_SIZE ** (-0.5)
    positions = shard_index * positions_here + jnp.arange(positions_here, dtype=jnp.int32)
    limit_pos = hist_lengths[:, None] + 1 + jnp.arange(tokens, dtype=jnp.int32)[None, :]
    usable = (positions[None, None, :] < limit_pos[:, :, None])[:, None, None]
    scores = jnp.where(usable, scores, MASKED_SCORE)
    highest = jnp.max(scores, axis=-1)
    weights = jnp.where(usable, jnp.exp(scores - highest[..., None]), 0.0)
    weight_sum = jnp.sum(weights, axis=-1)
    weighted = jnp.einsum(
        "shgtp,sphd->shgtd",
        weights.astype(jnp.bfloat16),
        heads_of_values,
        preferred_element_type=jnp.float32,
    )
    own_streams = streams // context_size
    highest, weight_sum, weighted = merged(
        (highest, weight_sum, weighted), "context", combine_partial
    )
    first_stream = shard_index * own_streams
    highest = lax.dynamic_slice_in_dim(highest, first_stream, own_streams, 0)
    weight_sum = lax.dynamic_slice_in_dim(weight_sum, first_stream, own_streams, 0)
    weighted = lax.dynamic_slice_in_dim(weighted, first_stream, own_streams, 0)
    result = weighted / weight_sum[..., None]
    return (
        result.transpose(0, 3, 1, 2, 4).reshape(own_streams, tokens, width_all).astype(jnp.bfloat16)
    )


def local(
    turn_q,
    new_turn_keys,
    new_turn_values,
    block_mask,
    query_dec,
    cache_keys,
    stream_cache_values,
    hist_lengths,
):
    turn_out = turn_attention(turn_q, new_turn_keys, new_turn_values, block_mask)
    stream_out = stream_attention(query_dec, cache_keys, stream_cache_values, hist_lengths)
    return (turn_out, stream_out)


def solution(mesh):
    in_specs = (
        P(("dp", "context"), "tensor"),
        P(("dp", "context"), "tensor"),
        P(("dp", "context"), "tensor"),
        P(),
        P("dp", None, "tensor"),
        P("dp", "context", "tensor"),
        P("dp", "context", "tensor"),
        P("dp"),
    )
    out_specs = (P(("dp", "context"), "tensor"), P(("dp", "context"), None, "tensor"))
    return jax.shard_map(local, mesh=mesh, in_specs=in_specs, out_specs=out_specs, check_vma=False)
```

profile of v0, /device:TPU:88, one launch (start us, length us, event | category | flops | bytes accessed | tf_op | source)
XLA Modules:
  0.0 334.9 jit_solution(14240453920623979347)
XLA Ops:
  8.7 1.0 reshape.327
  10.6 3.9 %fusion.33 = (f32[16,8,4]{1,2,0:T(4,128)S(1)}, f32[16,1024,4,8]{1,3,2,0:T(8,128)S(1)}) fusion(pred[16,4,1024]{2,1,0:T(4,128)(4,1)S(1)} %broadcast_compare_fusion.2, bf16[16,4,8,128]{3,2,1,0:T(8,128)(2,1)S(1)} %reshape.327, bf16[16,1024,128]{2,1,0:T(8,128)(2,1)} %param.19), kind=kOutput, calls=%fused_computation.58 | convolution fusion | flops 135790080 | bytes 6490112 | tf_op jit(solution)/shard_map/sthgd,sphd->shgtp/dot_general | solution.py:162
  14.5 1.6 fusion.36
  18.5 38.8 %all-gather = bf16[256,8,4]{1,2,0:T(4,128)(2,1)S(1)} all-gather(bf16[16,8,4]{1,2,0:T(4,128)(2,1)S(1)} %convert_element_type.182), channel_id=2, replica_groups=mesh['context'=16,'tensor'=8,'dp'=2] {'context'}, dimensions={0}, use_global_device_ids=true | all-gather | bytes 17408 | tf_op jit(solution)/shard_map/all_gather | solution.py:18
  57.4 37.7 %all-gather.1 = bf16[256,8,4]{1,2,0:T(4,128)(2,1)S(1)} all-gather(bf16[16,8,4]{1,2,0:T(4,128)(2,1)S(1)} %fusion.35), channel_id=3, replica_groups=mesh['context'=16,'tensor'=8,'dp'=2] {'context'}, dimensions={0}, use_global_device_ids=true | all-gather | bytes 17408 | tf_op jit(solution)/shard_map/all_gather | solution.py:18
  95.2 0.9 copy.64
  96.1 0.8 copy.65
  97.0 83.3 %all-gather.9.cloned.1.call-done = bf16[8192,128]{1,0:T(8,128)(2,1)} async-done(((bf16[512,128]{1,0:T(8,128)(2,1)}), bf16[8192,128]{1,0:T(8,128)(2,1)}) %all-gather.9.cloned.1.call-update) | async-done | bytes 2097168 | tf_op jit(solution)/shard_map/all_gather | solution.py:129
  180.4 91.1 %while.35 = (s32[]{:T(128)}, f32[1,8,512]{2,1,0:T(8,128)S(1)}, f32[1,8,512]{2,1,0:T(8,128)S(1)}, f32[1,8,512,128]{3,2,1,0:T(8,128)S(1)}, s32[16]{0:T(128)S(1)}, ...) while((s32[]{:T(128)}, f32[1,8,512]{2,1,0:T(8,128)S(1)}, ...), condition=%wide.region_7.8_spmd, body=%wide.region_0.7_spmd.sunk | while | flops 1103156224 | bytes 32001396 | solution.py:107
  181.8 1.0 fusion.62
  183.4 8.6 %conditional.2 = ((f32[1,8,512]{2,1,0:T(8,128)S(1)}, f32[1,8,512]{2,1,0:T(8,128)S(1)}, f32[1,8,512,128]{3,2,1,0:T(8,128)S(1)})) conditional(s32[]{:T(128)} %convert_element_type.224, (f32[1,8,512]{2,1,0:T(8,128)S(1)}, f32[1,8,512]{2,1,0:T(8,128)S(1)}, f32[1,8,512,128]{3,2,1,0:T(8,128)S(1)}) %tuple.95, (pred[512,512]{0,1:T(8,128)(4,1)S(1)}, ...), branch_computations={%region_3.3_spmd, %region_4.6_spmd} | conditional | flops 1102065664 | bytes 31720480 | solution.py:81
  183.4 2.4 fusion
  185.9 2.0 fusion.2
  188.0 4.0 %bitcast_add_fusion = f32[1,8,512,128]{3,2,1,0:T(8,128)S(1)} fusion(f32[1,8,512,128]{3,2,1,0:T(8,128)S(1)} %get-tuple-element.374, f32[512,512,8]{1,0,2:T(8,128)S(1)} %get-tuple-element.519, f32[8,512]{1,0:T(8,128)S(1)} %bitcast.147, pred[512,512]{0,1:T(8,128)(4,1)S(1)} %get-tuple-element.369, f32[8,512]{1,0:T(8,128)S(1)} %get-tuple-element.512, ...), kind=kOutput, calls=%fused_computation.8 | convolution fusion | flops 548405248 | bytes 13009408 | tf_op jit(solution)/shard_map/while/body/eval_jaxpr/cond/branch_1_fun/hgqk,khd->hgqd/dot_general | solution.py:70
  193.4 1.0 fusion.62
  196.4 1.0 fusion.62
  199.4 1.0 fusion.62
  202.4 1.0 fusion.62
  205.5 1.0 fusion.62
  208.5 1.0 fusion.62
  211.5 1.0 fusion.62
  213.1 8.6 %conditional.2 = ((f32[1,8,512]{2,1,0:T(8,128)S(1)}, f32[1,8,512]{2,1,0:T(8,128)S(1)}, f32[1,8,512,128]{3,2,1,0:T(8,128)S(1)})) conditional(s32[]{:T(128)} %convert_element_type.224, (f32[1,8,512]{2,1,0:T(8,128)S(1)}, f32[1,8,512]{2,1,0:T(8,128)S(1)}, f32[1,8,512,128]{3,2,1,0:T(8,128)S(1)}) %tuple.95, (pred[512,512]{0,1:T(8,128)(4,1)S(1)}, ...), branch_computations={%region_3.3_spmd, %region_4.6_spmd} | conditional | flops 1102065664 | bytes 31720480 | solution.py:81
  213.1 2.4 fusion
  215.5 2.0 fusion.2
  217.6 4.0 %bitcast_add_fusion = f32[1,8,512,128]{3,2,1,0:T(8,128)S(1)} fusion(f32[1,8,512,128]{3,2,1,0:T(8,128)S(1)} %get-tuple-element.374, f32[512,512,8]{1,0,2:T(8,128)S(1)} %get-tuple-element.519, f32[8,512]{1,0:T(8,128)S(1)} %bitcast.147, pred[512,512]{0,1:T(8,128)(4,1)S(1)} %get-tuple-element.369, f32[8,512]{1,0:T(8,128)S(1)} %get-tuple-element.512, ...), kind=kOutput, calls=%fused_computation.8 | convolution fusion | flops 548405248 | bytes 13009408 | tf_op jit(solution)/shard_map/while/body/eval_jaxpr/cond/branch_1_fun/hgqk,khd->hgqd/dot_general | solution.py:70
  223.1 1.0 fusion.62
  224.7 8.6 %conditional.2 = ((f32[1,8,512]{2,1,0:T(8,128)S(1)}, f32[1,8,512]{2,1,0:T(8,128)S(1)}, f32[1,8,512,128]{3,2,1,0:T(8,128)S(1)})) conditional(s32[]{:T(128)} %convert_element_type.224, (f32[1,8,512]{2,1,0:T(8,128)S(1)}, f32[1,8,512]{2,1,0:T(8,128)S(1)}, f32[1,8,512,128]{3,2,1,0:T(8,128)S(1)}) %tuple.95, (pred[512,512]{0,1:T(8,128)(4,1)S(1)}, ...), branch_computations={%region_3.3_spmd, %region_4.6_spmd} | conditional | flops 1102065664 | bytes 31720480 | solution.py:81
  224.7 2.4 fusion
  227.1 2.0 fusion.2
  229.2 4.0 %bitcast_add_fusion = f32[1,8,512,128]{3,2,1,0:T(8,128)S(1)} fusion(f32[1,8,512,128]{3,2,1,0:T(8,128)S(1)} %get-tuple-element.374, f32[512,512,8]{1,0,2:T(8,128)S(1)} %get-tuple-element.519, f32[8,512]{1,0:T(8,128)S(1)} %bitcast.147, pred[512,512]{0,1:T(8,128)(4,1)S(1)} %get-tuple-element.369, f32[8,512]{1,0:T(8,128)S(1)} %get-tuple-element.512, ...), kind=kOutput, calls=%fused_computation.8 | convolution fusion | flops 548405248 | bytes 13009408 | tf_op jit(solution)/shard_map/while/body/eval_jaxpr/cond/branch_1_fun/hgqk,khd->hgqd/dot_general | solution.py:70
  234.6 1.0 fusion.62
  236.2 8.6 %conditional.2 = ((f32[1,8,512]{2,1,0:T(8,128)S(1)}, f32[1,8,512]{2,1,0:T(8,128)S(1)}, f32[1,8,512,128]{3,2,1,0:T(8,128)S(1)})) conditional(s32[]{:T(128)} %convert_element_type.224, (f32[1,8,512]{2,1,0:T(8,128)S(1)}, f32[1,8,512]{2,1,0:T(8,128)S(1)}, f32[1,8,512,128]{3,2,1,0:T(8,128)S(1)}) %tuple.95, (pred[512,512]{0,1:T(8,128)(4,1)S(1)}, ...), branch_computations={%region_3.3_spmd, %region_4.6_spmd} | conditional | flops 1102065664 | bytes 31720480 | solution.py:81
  236.3 2.4 fusion
  238.7 2.0 fusion.2
  240.8 4.0 %bitcast_add_fusion = f32[1,8,512,128]{3,2,1,0:T(8,128)S(1)} fusion(f32[1,8,512,128]{3,2,1,0:T(8,128)S(1)} %get-tuple-element.374, f32[512,512,8]{1,0,2:T(8,128)S(1)} %get-tuple-element.519, f32[8,512]{1,0:T(8,128)S(1)} %bitcast.147, pred[512,512]{0,1:T(8,128)(4,1)S(1)} %get-tuple-element.369, f32[8,512]{1,0:T(8,128)S(1)} %get-tuple-element.512, ...), kind=kOutput, calls=%fused_computation.8 | convolution fusion | flops 548405248 | bytes 13009408 | tf_op jit(solution)/shard_map/while/body/eval_jaxpr/cond/branch_1_fun/hgqk,khd->hgqd/dot_general | solution.py:70
  246.2 1.0 fusion.62
  247.8 8.6 %conditional.2 = ((f32[1,8,512]{2,1,0:T(8,128)S(1)}, f32[1,8,512]{2,1,0:T(8,128)S(1)}, f32[1,8,512,128]{3,2,1,0:T(8,128)S(1)})) conditional(s32[]{:T(128)} %convert_element_type.224, (f32[1,8,512]{2,1,0:T(8,128)S(1)}, f32[1,8,512]{2,1,0:T(8,128)S(1)}, f32[1,8,512,128]{3,2,1,0:T(8,128)S(1)}) %tuple.95, (pred[512,512]{0,1:T(8,128)(4,1)S(1)}, ...), branch_computations={%region_3.3_spmd, %region_4.6_spmd} | conditional | flops 1102065664 | bytes 31720480 | solution.py:81
  247.8 2.4 fusion
  250.3 2.0 fusion.2
  252.4 4.0 %bitcast_add_fusion = f32[1,8,512,128]{3,2,1,0:T(8,128)S(1)} fusion(f32[1,8,512,128]{3,2,1,0:T(8,128)S(1)} %get-tuple-element.374, f32[512,512,8]{1,0,2:T(8,128)S(1)} %get-tuple-element.519, f32[8,512]{1,0:T(8,128)S(1)} %bitcast.147, pred[512,512]{0,1:T(8,128)(4,1)S(1)} %get-tuple-element.369, f32[8,512]{1,0:T(8,128)S(1)} %get-tuple-element.512, ...), kind=kOutput, calls=%fused_computation.8 | convolution fusion | flops 548405248 | bytes 13009408 | tf_op jit(solution)/shard_map/while/body/eval_jaxpr/cond/branch_1_fun/hgqk,khd->hgqd/dot_general | solution.py:70
  257.8 1.0 fusion.62
  260.8 1.0 fusion.62
  263.8 1.0 fusion.62
  266.9 1.0 fusion.62
  269.9 1.0 fusion.62
  272.9 1.2 copy.83
  274.2 0.9 fusion.47
  275.2 52.2 %while.36 = (s32[]{:T(128)}, f32[16,1,8,4]{0,3,2,1:T(4,128)S(1)}, f32[16,1,8,4]{0,3,2,1:T(4,128)S(1)}, f32[16,1,8,4,128]{4,3,2,1,0:T(4,128)S(1)}, bf16[16,16,1,8...) while((s32[]{:T(128)}, f32[16,1,8,4]{0,3,2,1:T(4,128)S(1)}, ...), condition=%wide.region_11.12_spmd, body=%wide.region_10.11_spmd.sunk | while | flops 267269 | bytes 953499 | solution.py:30
  276.7 0.9 constant_dynamic-slice_fusion.4
  277.8 0.8 fusion.65
  280.1 0.9 constant_dynamic-slice_fusion.4
  283.6 0.9 constant_dynamic-slice_fusion.4
  287.1 0.9 constant_dynamic-slice_fusion.4
  290.6 0.9 constant_dynamic-slice_fusion.4
  294.1 0.9 constant_dynamic-slice_fusion.4
  297.6 0.9 constant_dynamic-slice_fusion.4
  301.0 0.9 constant_dynamic-slice_fusion.4
  304.5 0.9 constant_dynamic-slice_fusion.4
  308.0 0.9 constant_dynamic-slice_fusion.4
  311.5 0.9 constant_dynamic-slice_fusion.4
  315.0 0.9 constant_dynamic-slice_fusion.4
  318.4 0.9 constant_dynamic-slice_fusion.4
  321.9 0.9 constant_dynamic-slice_fusion.4
  325.4 0.9 constant_dynamic-slice_fusion.4
  (249 shorter events, 56.7 us)
Async XLA Ops:
  7.2 89.8 %copy-start = (s32[16,16]{1,0:T(8,128)S(1)}, s32[16,16]{1,0:T(8,128)}, u32[]{:S(2)}) copy-start(s32[16,16]{1,0:T(8,128)} %param.17) | copy-start | bytes 3076
  7.2 89.8 %all-gather.7.cloned.1.call-start = ((), (), s32[]{:S(2)}) async-start(), calls=%async_computation | async-start | bytes 2228224 | tf_op jit(solution)/shard_map/all_gather | solution.py:128
  7.9 172.4 %all-gather.9.cloned.1.call-start = ((), (), s32[]{:S(2)}) async-start(), calls=%async_computation.1 | async-start | bytes 2228224 | tf_op jit(solution)/shard_map/all_gather | solution.py:129
  8.7 265.5 %all-gather.11.cloned.1.call-start = ((), (), s32[]{:S(2)}) async-start(), calls=%async_computation.2 | async-start | bytes 2228224 | tf_op jit(solution)/shard_map/all_gather | solution.py:18
  10.6 3.9 %copy-start.2 = (bf16[16,1024,128]{2,1,0:T(8,128)(2,1)S(1)}, bf16[16,1024,128]{2,1,0:T(8,128)(2,1)}, u32[]{:S(2)}) copy-start(bf16[16,1024,128]{2,1,0:T(8,128)(2,1)} %param.20) | copy-start | bytes 12582916
  16.1 1.2 copy-start.1
Sparse Core Ops, SparseCore 0:
  10.6 85.4 all-gather.6
  98.7 81.5 all-gather.8
  182.9 82.2 all-gather.10
where the time goes:
time: 338 us; the launch traced here: 335 us
  waiting for transfers between devices  84.7 us (25%)
  blocking collectives  76.5 us (23%)
  other arithmetic  65.7 us (19%)
  matrix products  37.8 us (11%)
  local copies, waits for them, and re-layouts  34.3 us (10%)
  loops' own time  21.8 us (6%)
  between operations  13.9 us (4%)
    all_gather x1, waiting for transfers between devices, turn_attention(): lax.all_gather(new_turn_values, 'context', axis=0, tiled=True)  83.3 us
    all_gather x2, blocking collectives, merged(): lax.all_gather(a.astype(kind), axis)  76.5 us
    another operation x1, loops' own time, attend_block(): lax.scan(visitor, carried_state, (jnp.arange(pieces, dtype=jnp.int32), ke...  20.9 us
    dot_general x5, matrix products, attend_live(): jnp.einsum('hgqk,khd->hgqd', weights.astype(jnp.bfloat16), heads_of_value...  20.2 us
    reduce_or x16, other arithmetic, attend_rows(): jnp.any(usable)  15.3 us
    dynamic_slice x15, local copies, waits for them, and re-layouts, take(): lax.dynamic_index_in_dim(a, source, 0, False).astype(own.dtype)  13.8 us
    dot_general x5, matrix products, attend_live(): jnp.einsum('qhgd,khd->hgqk', query_matrix, heads_of_keys, preferred_eleme...  12.1 us
    add x15, other arithmetic, combine_partial(): earlier[2] * scale_one[..., None] + later[2] * scale_two[..., None]  11.9 us
  transfers between devices with their start and end apart: 3, of which 1 were waited for; matrix products, arithmetic and copies ran while one was open for 25% of the time, Pallas kernels for 0%

commit v1 on v0

v1 whole, which is shorter than its diff:
```python
import math

import jax
import jax.numpy as jnp
from jax import lax
from jax.experimental import pallas as pl
from jax.experimental.pallas import tpu as pltpu
from jax.sharding import PartitionSpec as P

HEAD = 128
HEADS = 8
BLOCK = 512
STREAMS = 16
TOKENS = 4
ROWS = HEADS * TOKENS
CTX = 16
RING = 8
VROWS = 144
PACK = 48
SCALE = HEAD**-0.5 * math.log2(math.e)
NEG = -1e30
F32, BF16 = jnp.float32, jnp.bfloat16
NT = (((1,), (1,)), ((), ()))
MESH = pl.DeviceIdType.MESH


def kernel(
    mask_ref, hist_ref, k_ref, v_ref, qd_ref, q_hbm, ck_hbm, cv_hbm,
    out_ref, sout_ref,
    qv, qt, kb, vt, acc, m_ref, s0, s1, x0, x1,
    ck, cv, d0, d1, e0, e1, part, got,
    local_sem, ss, rs, pss, prs,
):
    c = lax.axis_index("context")
    shard = ck_hbm.shape[1]

    q_copy = pltpu.make_async_copy(q_hbm, qv, local_sem.at[2, 0])
    q_copy.start()
    caches = []
    for s in range(STREAMS):
        pair = (
            pltpu.make_async_copy(ck_hbm.at[s], ck.at[s], local_sem.at[0, s]),
            pltpu.make_async_copy(cv_hbm.at[s], cv.at[s], local_sem.at[1, s]),
        )
        caches.append(pair)

    barrier = pltpu.get_barrier_semaphore()
    for k in range(1, CTX):
        pl.semaphore_signal(
            barrier, inc=1, device_id={"context": lax.rem(c + k, CTX)}, device_id_type=MESH
        )
    vt[0, :HEAD, :] = v_ref[...].T
    vt[:, HEAD:, :] = jnp.ones((5, VROWS - HEAD, BLOCK), BF16)
    pl.semaphore_wait(barrier, CTX - 1)

    def k_at(slot):
        return k_ref if slot == 0 else kb.at[slot]

    def v_at(slot):
        return vt.at[slot, pl.ds(0, HEAD)]

    def send(what, slot, to, to_slot, sem):
        copy = pltpu.make_async_remote_copy(
            src_ref=k_at(slot) if what == 0 else v_at(slot),
            dst_ref=kb.at[to_slot] if what == 0 else v_at(to_slot),
            send_sem=ss.at[sem],
            recv_sem=rs.at[2 * to_slot + what],
            device_id={"context": to},
            device_id_type=MESH,
        )
        return copy

    def arrived(what, slot):
        send(what, slot, c, slot, 0).wait_recv()

    def first_block(stage):
        def at(index, stage_of, copies):
            if stage_of == stage:
                yield index, copies

        yield from at(0, 0, [(0, 0, 3, 3, 6), (1, 0, 3, 3, 7), (0, 0, 7, 4, 10), (0, 0, 6, 4, 11), (1, 0, 15, 4, 12), (1, 0, 14, 4, 13), (0, 0, 8, 4, 8), (1, 0, 8, 4, 9)])
        yield from at(1, 1, [(0, 1, 9, 4, 6), (1, 1, 9, 4, 7)])
        yield from at(6, 1, [(0, 4, 4, 4, 6), (0, 4, 5, 4, 7), (0, 4, 14, 4, 8)])
        yield from at(14, 1, [(1, 4, 12, 4, 6), (1, 4, 13, 4, 7), (1, 4, 6, 4, 8)])
        yield from at(7, 1, [(0, 4, 15, 4, 6)])
        yield from at(15, 1, [(1, 4, 7, 4, 6)])
        yield from at(2, 2, [(0, 2, 10, 4, 6), (1, 2, 10, 4, 7)])
        yield from at(3, 2, [(0, 3, 11, 4, 6), (1, 3, 11, 4, 7)])
        yield from at(5, 2, [(0, 4, 13, 4, 6)])
        yield from at(13, 2, [(1, 4, 5, 4, 6)])
        yield from at(4, 2, [(0, 4, 12, 4, 6)])
        yield from at(12, 2, [(1, 4, 4, 4, 6)])

    def start_first(stage):
        for index, copies in first_block(stage):

            @pl.when(c == index)
            def _(copies=copies):
                waited = set()
                for what, slot, to, to_slot, sem in copies:
                    if slot >= 3 and (what, slot) not in waited:
                        waited.add((what, slot))
                        arrived(what, slot)
                    send(what, slot, to, to_slot, sem).start()

    def wait_first():
        for stage in range(3):
            for index, copies in first_block(stage):

                @pl.when(c == index)
                def _(copies=copies):
                    for what, slot, to, to_slot, sem in copies:
                        send(what, slot, to, to_slot, sem).wait_send()

    nxt = jnp.minimum(c + 1, CTX - 1)

    def forward(slot, lowest, waits):
        for what in range(2):
            if waits:

                @pl.when(c >= slot)
                def _():
                    arrived(what, slot)

            if slot < 3:

                @pl.when((c >= lowest) & (c < CTX - 1))
                def _():
                    send(what, slot, nxt, slot + 1, 2 * slot + what).start()

    forward(0, 0, False)
    start_first(0)

    for k_copy, v_copy in caches:
        k_copy.start()
        v_copy.start()
    q_copy.wait()
    for h in range(HEADS):
        head = qv[:, h * HEAD : (h + 1) * HEAD].astype(F32) * SCALE
        qt[h] = head.astype(BF16).T

    sb, xb = (s0, s1), (x0, x1)

    def scores(slot, h, diagonal):
        s = jnp.dot(k_at(slot)[...], qt[h], preferred_element_type=F32)
        if diagonal:
            key = lax.broadcasted_iota(jnp.int32, s.shape, 0)
            query = lax.broadcasted_iota(jnp.int32, s.shape, 1)
            s = jnp.where(key <= query, s, NEG)
        sb[h % 2][...] = s
        xb[h % 2][...] = jnp.max(s, axis=0, keepdims=True)

    def weigh(slot, h, bias):
        top = xb[h % 2][...]
        if bias is None:
            new = shift = top
        else:
            old = m_ref[h, :1, :]
            new = jnp.maximum(old, top + bias)
            shift = new - bias
        p = jnp.exp2(sb[h % 2][...] - shift).astype(BF16)
        pv = jnp.dot(vt[slot], p, preferred_element_type=F32)
        if bias is None:
            acc[h] = pv
        else:
            acc[h] = acc[h] * jnp.exp2(old - new) + pv
        m_ref[h, :1, :] = new

    def attend(slot, bias, diagonal=False):
        scores(slot, 0, diagonal)
        for h in range(HEADS):
            if h + 1 < HEADS:
                scores(slot, h + 1, diagonal)
            weigh(slot, h, bias)

    def attend_slot(slot):
        column = jnp.maximum(c - slot, 0) if slot < 4 else 0
        bias = jnp.where(mask_ref[c, column] > 0, 0.0, NEG)

        @pl.when(c >= slot)
        def _():
            attend(slot, bias)

    attend(0, None, True)

    db, eb = (d0, d1), (e0, e1)
    col = lax.broadcasted_iota(jnp.int32, (ROWS, shard), 1)
    token = lax.rem(lax.broadcasted_iota(jnp.int32, (ROWS, shard), 0), TOKENS)
    ahead = col - token
    eye = lax.broadcasted_iota(jnp.int32, (ROWS, HEAD), 0) == lax.broadcasted_iota(
        jnp.int32, (ROWS, HEAD), 1
    )
    line = lax.broadcasted_iota(jnp.int32, (PACK - ROWS, HEAD), 0)

    def stream_scores(s, b):
        pltpu.make_async_copy(ck_hbm.at[s], ck.at[s], local_sem.at[0, s]).wait()
        rows = qd_ref[s].astype(F32) * SCALE
        rows = jnp.concatenate(
            [rows[:, g * HEAD : (g + 1) * HEAD] for g in range(HEADS)], axis=0
        ).astype(BF16)
        x = lax.dot_general(rows, ck[s], NT, preferred_element_type=F32)
        limit = hist_ref[s] + 1 - c * shard
        x = jnp.where(ahead < limit, x, NEG)
        db[b][...] = x
        eb[b][...] = jnp.broadcast_to(jnp.max(x, axis=1, keepdims=True), (ROWS, HEAD))

    def stream_weigh(s, b):
        pltpu.make_async_copy(cv_hbm.at[s], cv.at[s], local_sem.at[1, s]).wait()
        top = eb[b][:, :1]
        p = jnp.exp2(db[b][...] - top)
        total = jnp.sum(p, axis=1, keepdims=True)
        o = jnp.dot(p.astype(BF16), cv[s], preferred_element_type=F32) / total
        part[s, :ROWS, :] = o.astype(BF16)
        level = top + jnp.log(total) * math.log2(math.e)
        level = jnp.sum(jnp.where(eye, level, 0.0), axis=0, keepdims=True)
        high = level.astype(BF16).astype(F32)
        mid = (level - high).astype(BF16).astype(F32)
        low = level - high - mid
        packed = jnp.where(line == 0, high, jnp.where(line == 1, mid, jnp.where(line == 2, low, 0.0)))
        part[s, ROWS:, :] = packed.astype(BF16)

    stream_scores(0, 0)

    def streams(i, carry):
        for u in range(4):
            s = i * 4 + u
            stream_scores(s + 1, (u + 1) % 2)
            stream_weigh(s, u % 2)
        return carry

    lax.fori_loop(0, STREAMS // 4 - 1, streams, 0)
    for s in range(STREAMS - 4, STREAMS):
        if s + 1 < STREAMS:
            stream_scores(s + 1, (s + 1) % 2)
        stream_weigh(s, s % 2)

    forward(1, 1, True)
    start_first(1)

    def partial(k):
        to = lax.rem(c + k, CTX)
        return pltpu.make_async_remote_copy(
            src_ref=part.at[to],
            dst_ref=got.at[c],
            send_sem=pss.at[k],
            recv_sem=prs.at[k],
            device_id={"context": to},
            device_id_type=MESH,
        )

    for k in range(1, CTX):
        partial(k).start()
    got[c] = part[c]

    attend_slot(1)
    forward(2, 3, True)
    start_first(2)
    attend_slot(2)

    for what in range(2):
        kept = (c == 4) | (c == 5) | (c == 6) | (c == 7) | (c >= 8)
        taken = (
            (c == 6) | (c == 7) | (c == 4) | (c == 5)
            if what == 0
            else (c == 14) | (c == 15) | (c == 12) | (c == 13)
        )

        @pl.when(kept & jnp.logical_not(taken))
        def _():
            arrived(what, 4)

    attend_slot(4)

    for what in range(2):

        @pl.when((c >= 3) & (c != 3))
        def _():
            arrived(what, 3)

    attend_slot(3)

    for h in range(HEADS):
        o = acc[h, :HEAD, :] / acc[h, HEAD : HEAD + 1, :]
        out_ref[:, h * HEAD : (h + 1) * HEAD] = o.astype(BF16).T

    for k in range(1, CTX):
        partial(k).wait()

    def level_of(source):
        rows = got[source, ROWS:, :].astype(F32)
        row = rows[0:1, :] + rows[1:2, :] + rows[2:3, :]
        return jnp.sum(jnp.where(eye, row, 0.0), axis=1, keepdims=True)

    levels = [level_of(source) for source in range(CTX)]
    top = levels[0]
    for level in levels[1:]:
        top = jnp.maximum(top, level)
    total = jnp.zeros((ROWS, 1), F32)
    value = jnp.zeros((ROWS, HEAD), F32)
    for source, level in enumerate(levels):
        w = jnp.exp2(level - top)
        total += w
        value += got[source, :ROWS, :].astype(F32) * w
    value = value / total
    for g in range(HEADS):
        sout_ref[0, :, g * HEAD : (g + 1) * HEAD] = value[g * TOKENS : (g + 1) * TOKENS, :].astype(BF16)

    for slot in range(3):
        lowest = (0, 1, 3)[slot]
        for what in range(2):

            @pl.when((c >= lowest) & (c < CTX - 1))
            def _():
                send(what, slot, nxt, slot + 1, 2 * slot + what).wait_send()

    wait_first()


def local(turn_q, keys, values, block_mask, query_dec, cache_keys, cache_values, lengths):
    vmem = pl.BlockSpec(memory_space=pltpu.VMEM)
    smem = pl.BlockSpec(memory_space=pltpu.SMEM)
    anywhere = pl.BlockSpec(memory_space=pl.ANY)
    streams, shard, _ = cache_keys.shape
    return pl.pallas_call(
        kernel,
        out_shape=(
            jax.ShapeDtypeStruct(turn_q.shape, BF16),
            jax.ShapeDtypeStruct((1, TOKENS, HEADS * HEAD), BF16),
        ),
        in_specs=[smem, smem, vmem, vmem, vmem, anywhere, anywhere, anywhere],
        out_specs=(vmem, vmem),
        scratch_shapes=[
            pltpu.VMEM((BLOCK, HEADS * HEAD), BF16),
            pltpu.VMEM((HEADS, HEAD, BLOCK), BF16),
            pltpu.VMEM((5, BLOCK, HEAD), BF16),
            pltpu.VMEM((5, VROWS, BLOCK), BF16),
            pltpu.VMEM((HEADS, VROWS, BLOCK), F32),
            pltpu.VMEM((HEADS, 8, BLOCK), F32),
            pltpu.VMEM((BLOCK, BLOCK), F32),
            pltpu.VMEM((BLOCK, BLOCK), F32),
            pltpu.VMEM((1, BLOCK), F32),
            pltpu.VMEM((1, BLOCK), F32),
            pltpu.VMEM((streams, shard, HEAD), BF16),
            pltpu.VMEM((streams, shard, HEAD), BF16),
            pltpu.VMEM((ROWS, shard), F32),
            pltpu.VMEM((ROWS, shard), F32),
            pltpu.VMEM((ROWS, HEAD), F32),
            pltpu.VMEM((ROWS, HEAD), F32),
            pltpu.VMEM((streams, PACK, HEAD), BF16),
            pltpu.VMEM((CTX, PACK, HEAD), BF16),
            pltpu.SemaphoreType.DMA((3, STREAMS)),
            pltpu.SemaphoreType.DMA((14,)),
            pltpu.SemaphoreType.DMA((10,)),
            pltpu.SemaphoreType.DMA((CTX,)),
            pltpu.SemaphoreType.DMA((CTX,)),
        ],
        compiler_params=pltpu.CompilerParams(
            collective_id=0, has_side_effects=True, vmem_limit_bytes=56 * 2**20
        ),
        cost_estimate=pl.CostEstimate(
            flops=6 * 10**9, bytes_accessed=11 * 2**20, transcendentals=11 * 10**6
        ),
    )(block_mask, lengths, keys, values, query_dec, turn_q, cache_keys, cache_values)


def solution(mesh):
    in_specs = (
        P(("dp", "context"), "tensor"),
        P(("dp", "context"), "tensor"),
        P(("dp", "context"), "tensor"),
        P(),
        P("dp", None, "tensor"),
        P("dp", "context", "tensor"),
        P("dp", "context", "tensor"),
        P("dp"),
    )
    out_specs = (P(("dp", "context"), "tensor"), P(("dp", "context"), None, "tensor"))
    return jax.shard_map(local, mesh=mesh, in_specs=in_specs, out_specs=out_specs, check_vma=False)
```

time: 338 us -> 48.8 us (0.14)
  waiting for transfers between devices: 84.7 us -> 0 us
  blocking collectives: 76.5 us -> 0 us
  other arithmetic: 65.7 us -> 0 us
  Pallas kernels: 0 us -> 44.4 us
  matrix products: 37.8 us -> 0 us
  local copies, waits for them, and re-layouts: 34.3 us -> 3.56 us
  loops' own time: 21.8 us -> 0 us
  between operations: 13.9 us -> 0.64 us
    all_gather x3 -> x0, waiting for transfers between devices: 83.3 us -> none  [the longest x1 83.3 us: turn_attention(): lax.all_gather(new_turn_values, 'context', axis=0, tiled=True)]
    all_gather x2 -> x0, blocking collectives: 76.5 us -> none  [merged(): lax.all_gather(a.astype(kind), axis)]
    pallas_call x0 -> x1, Pallas kernels: none -> 44.4 us  [local(): pl.pallas_call(kernel, out_shape=(jax.ShapeDtypeStruct(turn_q.shape, BF16...]
    dot_general x12 -> x0, matrix products: 37.8 us -> none  [the longest x5 20.2 us: attend_live(): jnp.einsum('hgqk,khd->hgqd', weights.astype(jnp.bfloat16), heads_of_value...]
    dynamic_slice x33 -> x0, local copies, waits for them, and re-layouts: 23.6 us -> none  [the longest x15 13.8 us: take(): lax.dynamic_index_in_dim(a, source, 0, False).astype(own.dtype)]
    mul x35 -> x0, other arithmetic: 22.1 us -> none  [the longest x15 11.3 us: combine_partial(): later[2] * scale_two[..., None]]
    another operation x18 -> x0, loops' own time: 21.8 us -> none  [the longest x1 20.9 us: attend_block(): lax.scan(visitor, carried_state, (jnp.arange(pieces, dtype=jnp.int32), ke...]
    reduce_or x16 -> x0, other arithmetic: 15.3 us -> none  [attend_rows(): jnp.any(usable)]
  transfers between devices with their start and end apart: 3 -> 0, of which waited for: 1 -> 0; matrix products, arithmetic and copies ran while one was open for 25% -> 0% of each run, Pallas kernels for 0% -> 0%
where the time goes in v1:
time: 48.8 us; the launch traced here: 48.6 us
  Pallas kernels  44.4 us (91%)
  local copies, waits for them, and re-layouts  3.56 us (7%)
  between operations  0.64 us (1%)
    pallas_call x1, Pallas kernels, local(): pl.pallas_call(kernel, out_shape=(jax.ShapeDtypeStruct(turn_q.shape, BF16...  44.4 us
    unnamed x2, local copies, waits for them, and re-layouts  3.56 us

profile of v1, /device:TPU:88, one launch (start us, length us, event | category | flops | bytes accessed | tf_op | source)
XLA Modules:
  0.0 48.6 jit_solution(7459370773379793746)
XLA Ops:
  0.6 44.4 %shard_map.95 = (bf16[512,1024]{1,0:T(8,128)(2,1)}, bf16[1,4,1024]{2,1,0:T(4,128)(2,1)}) custom-call(s32[16,16]{1,0:T(8,128)} %mask_ref.1, s32[16]{0:T(128)} %hist_ref.1, bf16[512,128]{1,0:T(8,128)(2,1)} %k_ref.1, bf16[512,128]{1,0:T(8,128)(2,1)} %v_ref.1, bf16[16,4,1024]{2,1,0:T(4,128)(2,1)} %qd_ref.1, bf16[512,1024]{1,0:T(8,128)(2,1)} %q_hbm.1, ...), custom_call_target="tpu_custom_call" | custom-call | flops 6000000000 | bytes 11534336 | tf_op jit(solution)/shard_map/pallas_call | solution.py:324
  45.0 2.3 %copy.12 = bf16[512,1024]{1,0:T(8,128)(2,1)} copy(bf16[512,1024]{1,0:T(8,128)(2,1)} %get-tuple-element.4) | data formatting | bytes 2097152
  47.3 1.3 %copy.13 = bf16[1,4,1024]{2,1,0:T(4,128)(2,1)} copy(bf16[1,4,1024]{2,1,0:T(4,128)(2,1)} %get-tuple-element.5) | data formatting | bytes 16384

commit v2 on v1

v2 whole, which is shorter than its diff:
```python
import math

import jax
import jax.numpy as jnp
from jax import lax
from jax.experimental import pallas as pl
from jax.experimental.pallas import tpu as pltpu
from jax.sharding import PartitionSpec as P

HEAD = 128
HEADS = 8
BLOCK = 512
STREAMS = 16
TOKENS = 4
ROWS = HEADS * TOKENS
CTX = 16
RING = 8
VROWS = 144
PACK = 48
GROUP = 4
LOG2E = math.log2(math.e)
SCALE = HEAD**-0.5 * LOG2E
NEG = -1e30
F32, BF16 = jnp.float32, jnp.bfloat16
NT = (((1,), (1,)), ((), ()))
MESH = pl.DeviceIdType.MESH


def kernel(
    mask_ref, hist_ref, k_ref, v_ref, qd_ref, q_hbm, ck_hbm, cv_hbm,
    out_ref, sout_ref,
    qv, qt, vown, km, vm, k0, v0, acc, m_ref, s0, s1, x0, x1,
    ck, cv, d0, d1, e0, e1, tops, totals, part, pair, got,
    local_sem, ss, rs, pss, prs,
):
    c = lax.axis_index("context")
    z = lax.rem(c, RING)
    half = c - z
    other = RING - half
    shard = ck_hbm.shape[1]

    q_copy = pltpu.make_async_copy(q_hbm, qv, local_sem.at[2, 0])
    q_copy.start()
    groups = STREAMS // GROUP

    def cache_copy(which, g):
        here, there = ((ck_hbm, ck), (cv_hbm, cv))[which]
        some = pl.ds(g * GROUP, GROUP)
        return pltpu.make_async_copy(here.at[some], there.at[some], local_sem.at[which, g])

    for ref in (vown, vm, v0):
        index = (Ellipsis, pl.ds(HEAD, VROWS - HEAD), slice(None))
        ref[index] = jnp.ones(ref.shape[:-2] + (VROWS - HEAD, ref.shape[-1]), BF16)

    barrier = pltpu.get_barrier_semaphore()
    for k in range(1, CTX):
        pl.semaphore_signal(
            barrier, inc=1, device_id={"context": lax.rem(c + k, CTX)}, device_id_type=MESH
        )
    vown[:HEAD, :] = v_ref[...].T
    pl.semaphore_wait(barrier, CTX - 1)

    own = (k_ref, vown.at[pl.ds(0, HEAD)])

    def main(what, slot):
        return (km.at[slot - 1], vm.at[slot - 1, pl.ds(0, HEAD)])[what], 2 * (slot - 1) + what

    def zero(what):
        return (k0, v0.at[pl.ds(0, HEAD)])[what], 6 + what

    def copy(source, target, to, sem):
        return pltpu.make_async_remote_copy(
            src_ref=source,
            dst_ref=target[0],
            send_sem=ss.at[sem],
            recv_sem=rs.at[target[1]],
            device_id={"context": to},
            device_id_type=MESH,
        )

    def arrived(target):
        copy(target[0], target, c, 0).wait_recv()

    sent = []

    def start(when, copies):
        @pl.when(when)
        def _():
            for one in copies:
                copy(*one).start()

        sent.append((when, copies))

    def both(make):
        return [make(what) for what in range(2)]

    def await_when(when, targets):
        @pl.when(when)
        def _():
            for target in targets:
                arrived(target)

    nxt = jnp.minimum(c + 1, CTX - 1)

    start(c == 0, both(lambda w: (own[w], zero(w), 6, 6 + w)))
    start(c <= 14, both(lambda w: (own[w], main(w, 1), nxt, w)))
    start(c == 0, both(lambda w: (own[w], main(w, 3), 3, 8 + w)))
    start(c == 0, both(lambda w: (own[w], zero(w), 7, 10 + w)))

    def pass_on(when, slot):
        for w in range(2):
            await_when(c >= slot, [main(w, slot)])
            start(when, [(main(w, slot)[0], main(w, slot + 1), nxt, 2 * slot + w)])

    def first_to(when, what, targets):
        await_when(when, [zero(what)])
        start(when, [(zero(what)[0], zero(what), to, sem) for to, sem in targets])

    def first_both(when, to):
        for w in range(2):
            first_to(when, w, [(to, 6 + w)])

    def across(slot, to):
        start(c == slot, both(lambda w: (main(w, slot)[0], zero(w), to, 6 + w)))

    def stage_two():
        pass_on((c >= 1) & (c <= 14), 1)
        across(1, 9)
        first_to(c == 6, 0, [(4, 6)])

    def stage_three():
        first_to(c == 6, 1, [(4, 7)])
        start(c == 6, both(lambda w: (zero(w)[0], zero(w), 5, 8 + w)))
        start(c == 6, both(lambda w: (zero(w)[0], zero(w), 14, 10 + w)))

    def stage_four():
        pass_on((c >= 3) & (c <= 14), 2)
        across(2, 10)
        first_both(c == 9, 8)
        first_both(c == 7, 15)
        first_both(c == 4, 12)
        await_when(c == 3, both(lambda w: main(w, 3)))
        across(3, 11)

    def stage_five():
        first_both(c == 5, 13)

    for g in range(groups):
        cache_copy(0, g).start()
        cache_copy(1, g).start()
    q_copy.wait()

    sb, xb = (s0, s1), (x0, x1)

    def turn_head(h):
        head = qv[:, h * HEAD : (h + 1) * HEAD].astype(F32) * SCALE
        qt[h] = head.astype(BF16).T

    def scores(keys, h, diagonal):
        s = jnp.dot(keys[...], qt[h], preferred_element_type=F32)
        if diagonal:
            key = lax.broadcasted_iota(jnp.int32, s.shape, 0)
            query = lax.broadcasted_iota(jnp.int32, s.shape, 1)
            s = jnp.where(key <= query, s, NEG)
        sb[h % 2][...] = s
        xb[h % 2][...] = jnp.max(s, axis=0, keepdims=True)

    def weigh(values, bias, h):
        top = xb[h % 2][...]
        if bias is None:
            new = shift = top
        else:
            old = m_ref[h, :1, :]
            new = jnp.maximum(old, top + bias)
            shift = new - bias
        p = jnp.exp2(sb[h % 2][...] - shift).astype(BF16)
        pv = jnp.dot(values[...], p, preferred_element_type=F32)
        if bias is None:
            acc[h] = pv
        else:
            acc[h] = acc[h] * jnp.exp2(old - new) + pv
        m_ref[h, :1, :] = new

    def finish(h):
        o = acc[h, :HEAD, :] / acc[h, HEAD : HEAD + 1, :]
        out_ref[:, h * HEAD : (h + 1) * HEAD] = o.astype(BF16).T

    def attend(keys, values, bias, diagonal=False, last=False):
        if diagonal:
            turn_head(0)
        scores(keys, 0, diagonal)
        for h in range(HEADS):
            if h + 1 < HEADS:
                if diagonal:
                    turn_head(h + 1)
                scores(keys, h + 1, diagonal)
            weigh(values, bias, h)
            if last and h:
                finish(h - 1)
        if last:
            finish(HEADS - 1)

    def attend_main(slot, when, last=False):
        allowed = mask_ref[c, jnp.maximum(c - slot, 0)] > 0
        bias = jnp.where(allowed, 0.0, NEG)

        @pl.when(when)
        def _():
            attend(km.at[slot - 1], vm.at[slot - 1], bias, last=last)

    def attend_zero(when, last=False):
        bias = jnp.where(mask_ref[c, 0] > 0, 0.0, NEG)

        @pl.when(when)
        def _():
            attend(k0, v0, bias, last=last)

    db, eb = (d0, d1), (e0, e1)
    col = lax.broadcasted_iota(jnp.int32, (ROWS, shard), 1)
    token = lax.rem(lax.broadcasted_iota(jnp.int32, (ROWS, shard), 0), TOKENS)
    ahead = col - token
    eye = lax.broadcasted_iota(jnp.int32, (ROWS, HEAD), 0) == lax.broadcasted_iota(
        jnp.int32, (ROWS, HEAD), 1
    )
    line = lax.broadcasted_iota(jnp.int32, (PACK - ROWS, HEAD), 0)

    def stream_scores(s, b):
        rows = qd_ref[s].astype(F32) * SCALE
        rows = jnp.concatenate(
            [rows[:, g * HEAD : (g + 1) * HEAD] for g in range(HEADS)], axis=0
        ).astype(BF16)
        x = lax.dot_general(rows, ck[s], NT, preferred_element_type=F32)
        limit = hist_ref[s] + 1 - c * shard
        x = jnp.where(ahead < limit, x, NEG)
        db[b][...] = x
        eb[b][...] = jnp.broadcast_to(jnp.max(x, axis=1, keepdims=True), (ROWS, HEAD))

    def stream_weigh(s, b):
        top = eb[b][:, :1]
        p = jnp.exp2(db[b][...] - top)
        total = jnp.sum(p, axis=1, keepdims=True)
        o = jnp.dot(p.astype(BF16), cv[s], preferred_element_type=F32) / total
        part[s, :ROWS, :] = o.astype(BF16)
        tops[s] = eb[b][...]
        totals[s] = jnp.broadcast_to(total, (ROWS, HEAD))

    def store_level(ref, s, level):
        level = jnp.sum(jnp.where(eye, level, 0.0), axis=0, keepdims=True)
        high = level.astype(BF16).astype(F32)
        mid = (level - high).astype(BF16).astype(F32)
        low = level - high - mid
        packed = jnp.where(line == 0, high, jnp.where(line == 1, mid, jnp.where(line == 2, low, 0.0)))
        ref[s, ROWS:, :] = packed.astype(BF16)

    def level_of(ref, s):
        rows = ref[s, ROWS:, :].astype(F32)
        row = rows[0:1, :] + rows[1:2, :] + rows[2:3, :]
        return jnp.sum(jnp.where(eye, row, 0.0), axis=1, keepdims=True)

    def streams(first, groups_now):
        stream_scores(first, 0)

        def group(i, carry):
            for u in range(GROUP):
                s = first + i * GROUP + u
                if u + 1 < GROUP:
                    stream_scores(s + 1, (u + 1) % 2)
                else:
                    stream_scores(jnp.minimum(s + 1, STREAMS - 1), (u + 1) % 2)
                stream_weigh(s, u % 2)
            return carry

        lax.fori_loop(0, groups_now, group, 0)

    def cross_copy():
        return pltpu.make_async_remote_copy(
            src_ref=part.at[pl.ds(other, RING)],
            dst_ref=pair,
            send_sem=pss.at[0],
            recv_sem=prs.at[0],
            device_id={"context": lax.rem(c + RING, CTX)},
            device_id_type=MESH,
        )

    def merge_pairs():
        cross_copy().wait()
        for n in range(RING):
            s = half + n
            one, two = level_of(part, s), level_of(pair, n)
            top = jnp.maximum(one, two)
            w_one, w_two = jnp.exp2(one - top), jnp.exp2(two - top)
            total = w_one + w_two
            value = part[s, :ROWS, :].astype(F32) * w_one + pair[n, :ROWS, :].astype(F32) * w_two
            part[s, :ROWS, :] = (value / total).astype(BF16)
            store_level(part, s, top + jnp.log(total) * LOG2E)

    def ring_copy(k):
        to = half + lax.rem(z + k, RING)
        return pltpu.make_async_remote_copy(
            src_ref=part.at[to],
            dst_ref=got.at[z],
            send_sem=pss.at[k],
            recv_sem=prs.at[k],
            device_id={"context": to},
            device_id_type=MESH,
        )

    attend(k_ref, vown, None, True)
    for g in range(groups):
        cache_copy(0, g).wait()
        cache_copy(1, g).wait()
    streams(0, groups // 2)
    stage_two()
    streams(STREAMS // 2, groups // 2)
    stage_three()
    for s in range(STREAMS):
        store_level(part, s, tops[s] + jnp.log(totals[s]) * LOG2E)
    cross_copy().start()
    attend_main(1, c >= 1)
    stage_four()
    attend_main(2, c >= 2)
    stage_five()
    merge_pairs()
    for k in range(1, RING):
        ring_copy(k).start()
    got[z] = part[c]

    sooner = (c == 4) | (c == 6) | (c == 7) | (c == 9) | (c == 14)
    later = (c >= 4) & jnp.logical_not(sooner)
    await_when(c == 14, both(zero))
    attend_zero(sooner)
    await_when(c >= 4, both(lambda w: main(w, 3)))
    attend_main(3, sooner | (c == 3), True)
    attend_main(3, later)
    await_when(later & (c != 5), both(zero))
    attend_zero(later, True)

    @pl.when(c < 3)
    def _():
        for h in range(HEADS):
            finish(h)

    for k in range(1, RING):
        ring_copy(k).wait()
    levels = [level_of(got, n) for n in range(RING)]
    top = levels[0]
    for level in levels[1:]:
        top = jnp.maximum(top, level)
    total = jnp.zeros((ROWS, 1), F32)
    value = jnp.zeros((ROWS, HEAD), F32)
    for n, level in enumerate(levels):
        w = jnp.exp2(level - top)
        total += w
        value += got[n, :ROWS, :].astype(F32) * w
    value = value / total
    for g in range(HEADS):
        sout_ref[0, :, g * HEAD : (g + 1) * HEAD] = value[g * TOKENS : (g + 1) * TOKENS, :].astype(BF16)

    for when, some in sent:

        @pl.when(when)
        def _(some=some):
            for one in some:
                copy(*one).wait_send()


def local(turn_q, keys, values, block_mask, query_dec, cache_keys, cache_values, lengths):
    vmem = pl.BlockSpec(memory_space=pltpu.VMEM)
    smem = pl.BlockSpec(memory_space=pltpu.SMEM)
    anywhere = pl.BlockSpec(memory_space=pl.ANY)
    streams, shard, _ = cache_keys.shape
    return pl.pallas_call(
        kernel,
        out_shape=(
            jax.ShapeDtypeStruct(turn_q.shape, BF16),
            jax.ShapeDtypeStruct((1, TOKENS, HEADS * HEAD), BF16),
        ),
        in_specs=[smem, smem, vmem, vmem, vmem, anywhere, anywhere, anywhere],
        out_specs=(vmem, vmem),
        scratch_shapes=[
            pltpu.VMEM((BLOCK, HEADS * HEAD), BF16),
            pltpu.VMEM((HEADS, HEAD, BLOCK), BF16),
            pltpu.VMEM((VROWS, BLOCK), BF16),
            pltpu.VMEM((3, BLOCK, HEAD), BF16),
            pltpu.VMEM((3, VROWS, BLOCK), BF16),
            pltpu.VMEM((BLOCK, HEAD), BF16),
            pltpu.VMEM((VROWS, BLOCK), BF16),
            pltpu.VMEM((HEADS, VROWS, BLOCK), F32),
            pltpu.VMEM((HEADS, 8, BLOCK), F32),
            pltpu.VMEM((BLOCK, BLOCK), F32),
            pltpu.VMEM((BLOCK, BLOCK), F32),
            pltpu.VMEM((1, BLOCK), F32),
            pltpu.VMEM((1, BLOCK), F32),
            pltpu.VMEM((streams, shard, HEAD), BF16),
            pltpu.VMEM((streams, shard, HEAD), BF16),
            pltpu.VMEM((ROWS, shard), F32),
            pltpu.VMEM((ROWS, shard), F32),
            pltpu.VMEM((ROWS, HEAD), F32),
            pltpu.VMEM((ROWS, HEAD), F32),
            pltpu.VMEM((streams, ROWS, HEAD), F32),
            pltpu.VMEM((streams, ROWS, HEAD), F32),
            pltpu.VMEM((streams, PACK, HEAD), BF16),
            pltpu.VMEM((RING, PACK, HEAD), BF16),
            pltpu.VMEM((RING, PACK, HEAD), BF16),
            pltpu.SemaphoreType.DMA((3, STREAMS // GROUP)),
            pltpu.SemaphoreType.DMA((12,)),
            pltpu.SemaphoreType.DMA((8,)),
            pltpu.SemaphoreType.DMA((RING,)),
            pltpu.SemaphoreType.DMA((RING,)),
        ],
        compiler_params=pltpu.CompilerParams(
            collective_id=0, has_side_effects=True, vmem_limit_bytes=56 * 2**20
        ),
        cost_estimate=pl.CostEstimate(
            flops=6 * 10**9, bytes_accessed=11 * 2**20, transcendentals=11 * 10**6
        ),
    )(block_mask, lengths, keys, values, query_dec, turn_q, cache_keys, cache_values)


def solution(mesh):
    in_specs = (
        P(("dp", "context"), "tensor"),
        P(("dp", "context"), "tensor"),
        P(("dp", "context"), "tensor"),
        P(),
        P("dp", None, "tensor"),
        P("dp", "context", "tensor"),
        P("dp", "context", "tensor"),
        P("dp"),
    )
    out_specs = (P(("dp", "context"), "tensor"), P(("dp", "context"), None, "tensor"))
    return jax.shard_map(local, mesh=mesh, in_specs=in_specs, out_specs=out_specs, check_vma=False)
```

time: 48.8 us -> 42.9 us (0.88)
  Pallas kernels: 44.4 us -> 38.5 us
    pallas_call x1, Pallas kernels: 44.4 us -> 38.5 us  [local(): pl.pallas_call(kernel, out_shape=(jax.ShapeDtypeStruct(turn_q.shape, BF16...]
where the time goes in v2:
time: 42.9 us; the launch traced here: 42.7 us
  Pallas kernels  38.5 us (90%)
  local copies, waits for them, and re-layouts  3.56 us (8%)
  between operations  0.64 us (1%)
    pallas_call x1, Pallas kernels, local(): pl.pallas_call(kernel, out_shape=(jax.ShapeDtypeStruct(turn_q.shape, BF16...  38.5 us
    unnamed x2, local copies, waits for them, and re-layouts  3.56 us

profile of v2, /device:TPU:88, one launch (start us, length us, event | category | flops | bytes accessed | tf_op | source)
XLA Modules:
  0.0 42.7 jit_solution(14694943084514923374)
XLA Ops:
  0.6 38.5 %shard_map.95 = (bf16[512,1024]{1,0:T(8,128)(2,1)}, bf16[1,4,1024]{2,1,0:T(4,128)(2,1)}) custom-call(s32[16,16]{1,0:T(8,128)} %mask_ref.1, s32[16]{0:T(128)} %hist_ref.1, bf16[512,128]{1,0:T(8,128)(2,1)} %k_ref.1, bf16[512,128]{1,0:T(8,128)(2,1)} %v_ref.1, bf16[16,4,1024]{2,1,0:T(4,128)(2,1)} %qd_ref.1, bf16[512,1024]{1,0:T(8,128)(2,1)} %q_hbm.1, ...), custom_call_target="tpu_custom_call" | custom-call | flops 6000000000 | bytes 11534336 | tf_op jit(solution)/shard_map/pallas_call | solution.py:372
  39.2 2.3 %copy.12 = bf16[512,1024]{1,0:T(8,128)(2,1)} copy(bf16[512,1024]{1,0:T(8,128)(2,1)} %get-tuple-element.4) | data formatting | bytes 2097152
  41.4 1.3 %copy.13 = bf16[1,4,1024]{2,1,0:T(4,128)(2,1)} copy(bf16[1,4,1024]{2,1,0:T(4,128)(2,1)} %get-tuple-element.5) | data formatting | bytes 16384

commit v3 on v2

--- a/solution.py
+++ b/solution.py
@@ -48,6 +48,10 @@
         some = pl.ds(g * GROUP, GROUP)
         return pltpu.make_async_copy(here.at[some], there.at[some], local_sem.at[which, g])
 
+    for g in range(groups):
+        cache_copy(0, g).start()
+        cache_copy(1, g).start()
+
     for ref in (vown, vm, v0):
         index = (Ellipsis, pl.ds(HEAD, VROWS - HEAD), slice(None))
         ref[index] = jnp.ones(ref.shape[:-2] + (VROWS - HEAD, ref.shape[-1]), BF16)
@@ -58,7 +62,6 @@
             barrier, inc=1, device_id={"context": lax.rem(c + k, CTX)}, device_id_type=MESH
         )
     vown[:HEAD, :] = v_ref[...].T
-    pl.semaphore_wait(barrier, CTX - 1)
 
     own = (k_ref, vown.at[pl.ds(0, HEAD)])
 
@@ -102,15 +105,9 @@
 
     nxt = jnp.minimum(c + 1, CTX - 1)
 
-    start(c == 0, both(lambda w: (own[w], zero(w), 6, 6 + w)))
-    start(c <= 14, both(lambda w: (own[w], main(w, 1), nxt, w)))
-    start(c == 0, both(lambda w: (own[w], main(w, 3), 3, 8 + w)))
-    start(c == 0, both(lambda w: (own[w], zero(w), 7, 10 + w)))
-
-    def pass_on(when, slot):
-        for w in range(2):
-            await_when(c >= slot, [main(w, slot)])
-            start(when, [(main(w, slot)[0], main(w, slot + 1), nxt, 2 * slot + w)])
+    def pass_on(when, slot, w):
+        await_when(c >= slot, [main(w, slot)])
+        start(when, [(main(w, slot)[0], main(w, slot + 1), nxt, 2 * slot + w)])
 
     def first_to(when, what, targets):
         await_when(when, [zero(what)])
@@ -120,12 +117,13 @@
         for w in range(2):
             first_to(when, w, [(to, 6 + w)])
 
-    def across(slot, to):
-        start(c == slot, both(lambda w: (main(w, slot)[0], zero(w), to, 6 + w)))
+    def across(slot, to, w):
+        start(c == slot, [(main(w, slot)[0], zero(w), to, 6 + w)])
 
     def stage_two():
-        pass_on((c >= 1) & (c <= 14), 1)
-        across(1, 9)
+        pass_on((c >= 1) & (c <= 14), 1, 1)
+        across(1, 9, 0)
+        across(1, 9, 1)
         first_to(c == 6, 0, [(4, 6)])
 
     def stage_three():
@@ -133,22 +131,18 @@
         start(c == 6, both(lambda w: (zero(w)[0], zero(w), 5, 8 + w)))
         start(c == 6, both(lambda w: (zero(w)[0], zero(w), 14, 10 + w)))
 
+    def stage_one():
+        pass_on((c >= 1) & (c <= 14), 1, 0)
+
     def stage_four():
-        pass_on((c >= 3) & (c <= 14), 2)
-        across(2, 10)
-        first_both(c == 9, 8)
         first_both(c == 7, 15)
         first_both(c == 4, 12)
-        await_when(c == 3, both(lambda w: main(w, 3)))
-        across(3, 11)
+        for w in range(2):
+            await_when(c == 3, [main(w, 3)])
+            across(3, 11, w)
 
     def stage_five():
         first_both(c == 5, 13)
-
-    for g in range(groups):
-        cache_copy(0, g).start()
-        cache_copy(1, g).start()
-    q_copy.wait()
 
     sb, xb = (s0, s1), (x0, x1)
 
@@ -294,6 +288,12 @@
             part[s, :ROWS, :] = (value / total).astype(BF16)
             store_level(part, s, top + jnp.log(total) * LOG2E)
 
+    def share():
+        merge_pairs()
+        for k in range(1, RING):
+            ring_copy(k).start()
+        got[z] = part[c]
+
     def ring_copy(k):
         to = half + lax.rem(z + k, RING)
         return pltpu.make_async_remote_copy(
@@ -305,25 +305,82 @@
             device_id_type=MESH,
         )
 
-    attend(k_ref, vown, None, True)
-    for g in range(groups):
-        cache_copy(0, g).wait()
-        cache_copy(1, g).wait()
-    streams(0, groups // 2)
+    def diagonal():
+        q_copy.wait()
+        attend(k_ref, vown, None, True)
+
+    def decode(first):
+        if first == 0:
+            for g in range(groups):
+                cache_copy(0, g).wait()
+                cache_copy(1, g).wait()
+        streams(first, groups // 2)
+
+    def levels_of_all():
+        for s in range(STREAMS):
+            store_level(part, s, tops[s] + jnp.log(totals[s]) * LOG2E)
+
+    early = z <= 3
+    ahead_of_all = early | (c < RING)
+
+    @pl.when(ahead_of_all)
+    def _():
+        diagonal()
+
+    @pl.when(early)
+    def _():
+        decode(0)
+        decode(STREAMS // 2)
+        levels_of_all()
+
+    pl.semaphore_wait(barrier, CTX - 1)
+
+    for w in range(2):
+        start(c <= 14, [(own[w], main(w, 1), nxt, w)])
+        start(c == 0, [(own[w], zero(w), 6, 6 + w)])
+    start(c == 0, both(lambda w: (own[w], zero(w), 7, 8 + w)))
+
+    @pl.when(early)
+    def _():
+        cross_copy().start()
+
+    @pl.when(jnp.logical_not(ahead_of_all))
+    def _():
+        diagonal()
+
+    stage_one()
+
+    @pl.when(jnp.logical_not(early))
+    def _():
+        decode(0)
+
     stage_two()
-    streams(STREAMS // 2, groups // 2)
+
+    @pl.when(jnp.logical_not(early))
+    def _():
+        decode(STREAMS // 2)
+
     stage_three()
-    for s in range(STREAMS):
-        store_level(part, s, tops[s] + jnp.log(totals[s]) * LOG2E)
-    cross_copy().start()
+
+    @pl.when(jnp.logical_not(early))
+    def _():
+        levels_of_all()
+        cross_copy().start()
+
+    pass_on((c >= 2) & (c <= 14), 2, 0)
+    across(2, 10, 0)
+    first_to(c == 9, 0, [(8, 6)])
     attend_main(1, c >= 1)
+    first_to(c == 9, 1, [(8, 7)])
+    pass_on((c >= 2) & (c <= 14), 2, 1)
+    across(2, 10, 1)
+    @pl.when(c != 8)
+    def _():
+        share()
+
     stage_four()
     attend_main(2, c >= 2)
     stage_five()
-    merge_pairs()
-    for k in range(1, RING):
-        ring_copy(k).start()
-    got[z] = part[c]
 
     sooner = (c == 4) | (c == 6) | (c == 7) | (c == 9) | (c == 14)
     later = (c >= 4) & jnp.logical_not(sooner)
@@ -332,6 +389,11 @@
     await_when(c >= 4, both(lambda w: main(w, 3)))
     attend_main(3, sooner | (c == 3), True)
     attend_main(3, later)
+
+    @pl.when(c == 8)
+    def _():
+        share()
+
     await_when(later & (c != 5), both(zero))
     attend_zero(later, True)
 

time: 42.9 us -> 41.1 us (0.958)
  the two profiles are of different devices: /device:TPU:88 before, /device:TPU:126 now
where the time goes in v3:
time: 41.1 us; the launch traced here: 41 us
  Pallas kernels  36.7 us (89%)
  local copies, waits for them, and re-layouts  3.56 us (9%)
  between operations  0.64 us (2%)
    pallas_call x1, Pallas kernels, local(): pl.pallas_call(kernel, out_shape=(jax.ShapeDtypeStruct(turn_q.shape, BF16...  36.7 us
    unnamed x2, local copies, waits for them, and re-layouts  3.56 us

profile of v3, /device:TPU:126, one launch (start us, length us, event | category | flops | bytes accessed | tf_op | source)
XLA Modules:
  0.0 41.0 jit_solution(464905175860976665)
XLA Ops:
  0.6 36.7 %shard_map.95 = (bf16[512,1024]{1,0:T(8,128)(2,1)}, bf16[1,4,1024]{2,1,0:T(4,128)(2,1)}) custom-call(s32[16,16]{1,0:T(8,128)} %mask_ref.1, s32[16]{0:T(128)} %hist_ref.1, bf16[512,128]{1,0:T(8,128)(2,1)} %k_ref.1, bf16[512,128]{1,0:T(8,128)(2,1)} %v_ref.1, bf16[16,4,1024]{2,1,0:T(4,128)(2,1)} %qd_ref.1, bf16[512,1024]{1,0:T(8,128)(2,1)} %q_hbm.1, ...), custom_call_target="tpu_custom_call" | custom-call | flops 6000000000 | bytes 11534336 | tf_op jit(solution)/shard_map/pallas_call | solution.py:434
  37.4 2.3 %copy.12 = bf16[512,1024]{1,0:T(8,128)(2,1)} copy(bf16[512,1024]{1,0:T(8,128)(2,1)} %get-tuple-element.4) | data formatting | bytes 2097152
  39.6 1.3 %copy.13 = bf16[1,4,1024]{2,1,0:T(4,128)(2,1)} copy(bf16[1,4,1024]{2,1,0:T(4,128)(2,1)} %get-tuple-element.5) | data formatting | bytes 16384
